TPU v7x, 32 devices: a whole 2x2x4 slice. The times are simulated.
32 devices in a mesh: dp: 8 (over z, y), own: 4 (over x, core).
Axes of the slice: x: 2, y: 2, z: 4, core: 2. Of those that a mesh axis runs over, the one named last changes fastest.
Arguments:
- tokens: bfloat16 [8192, 2560], P('dp'), may hold values from -6 to 6
- route_w: float32 [8192, 2], P('dp'), may hold values from 0.1 to 1
- w_gate: bfloat16 [4, 2560, 768], P('own', 'dp'), may hold values from -0.125 to 0.125
- w_up: bfloat16 [4, 2560, 768], P('own', 'dp'), may hold values from -0.125 to 0.125
- slot_token: int32 [8, 4, 512], P('dp', 'own'), may hold values from 0 to 1023, as said below
- slot_pick: int32 [8, 4, 512], P('dp', 'own'), may hold values from 0 to 1
- live_blocks: int32 [8, 4], P('dp', 'own'), may hold values from 1 to 4, as said below
- d_hidden: bfloat16 [8, 4, 512, 768], P('dp', 'own'), may hold values from -6 to 6
Outputs:
- hidden: bfloat16 [8, 4, 512, 768], P('dp', 'own')
- grad_gate: float32 [4, 2560, 768], P('own', 'dp')
- grad_up: float32 [4, 2560, 768], P('own', 'dp')
- d_tokens: bfloat16 [8192, 2560], P(('dp', 'own'))
- d_route: float32 [8192, 2], P(('dp', 'own'))
Inputs may be any that keep to these rules, and one draw needn't show every extreme that they name: For each index of dp the pairs (slot_token, slot_pick) over all experts and all 512 slots are distinct. `live_blocks`: 4 is reached by some entry.
All inputs are finite; a program needn't handle non-finite values.
Results may differ from a plain program's by a relative error of at most 0.0052.
Values may be sent and summed in bfloat16 or wider, within the bound.
A program may use at most 128 MiB of HBM per device.

v0:
```python
import math

import jax
import jax.numpy as jnp
from jax import lax
from jax.sharding import PartitionSpec as P

BLK = 128


def finish(pre_gate, pre_up, block_gate, block_cot):
    sigmoid_gate = jax.nn.sigmoid(pre_gate)
    activated = pre_gate * sigmoid_gate
    block_hidden = (activated * pre_up * block_gate).astype(jnp.bfloat16)
    scaled_cot = block_cot * block_gate
    grad_pre = scaled_cot * pre_up * sigmoid_gate * (1.0 + pre_gate * (1.0 - sigmoid_gate))
    grad_up_pre = scaled_cot * activated
    grad_cat = jnp.concatenate(
        (grad_pre.astype(jnp.bfloat16), grad_up_pre.astype(jnp.bfloat16)), axis=1
    )
    route_grad = jnp.sum(block_cot * activated * pre_up, axis=1)
    return (block_hidden, grad_cat, route_grad)


def run_blocks(rows_x, gate_col, cot_all, w_full, live_count):
    capacity = rows_x.shape[0]
    hidden_width = w_full.shape[1] // 2
    initial = (
        jnp.zeros((capacity, hidden_width), jnp.bfloat16),
        jnp.zeros((capacity, 2 * hidden_width), jnp.bfloat16),
        jnp.zeros((capacity, w_full.shape[0]), jnp.float32),
        jnp.zeros((capacity,), jnp.float32),
    )

    def block_step(block_index, state_now):
        hidden, grad_cat, token_grad_rows, route_grad = state_now
        first = (block_index * BLK).astype(jnp.int32)
        block_rows = lax.dynamic_slice_in_dim(rows_x, first, BLK, 0)
        block_gate = lax.dynamic_slice_in_dim(gate_col, first, BLK, 0)[:, None]
        block_cot = lax.dynamic_slice_in_dim(cot_all, first, BLK, 0).astype(jnp.float32)
        projected = jnp.dot(block_rows, w_full, preferred_element_type=jnp.float32)
        block_hidden, block_dcat, block_route = finish(
            projected[:, :hidden_width], projected[:, hidden_width:], block_gate, block_cot
        )
        block_tgrad = lax.dot_general(
            block_dcat, w_full, (((1,), (1,)), ((), ())), preferred_element_type=jnp.float32
        )
        hidden = lax.dynamic_update_slice_in_dim(hidden, block_hidden, first, 0)
        grad_cat = lax.dynamic_update_slice_in_dim(grad_cat, block_dcat, first, 0)
        token_grad_rows = lax.dynamic_update_slice_in_dim(token_grad_rows, block_tgrad, first, 0)
        route_grad = lax.dynamic_update_slice_in_dim(route_grad, block_route, first, 0)
        return (hidden, grad_cat, token_grad_rows, route_grad)

    return lax.fori_loop(jnp.int32(0), jnp.asarray(live_count), block_step, initial)


def weight_sum(rows_x, grad_cat, live_count, offset, length):
    offset_index = jnp.asarray(offset).astype(jnp.int32)

    def add_block(block_index, running):
        first = (block_index * BLK).astype(jnp.int32)
        block_rows = lax.dynamic_slice(rows_x, (first, offset_index), (BLK, length))
        block_dcat = lax.dynamic_slice_in_dim(grad_cat, first, BLK, 0)
        return running + lax.dot_general(
            block_rows, block_dcat, (((0,), (0,)), ((), ())), preferred_element_type=jnp.float32
        )

    return lax.fori_loop(
        jnp.int32(0),
        jnp.asarray(live_count),
        add_block,
        jnp.zeros((length, grad_cat.shape[1]), jnp.float32),
    )


def shards(tokens, route_w, w_gate, w_up, slot_token, slot_pick, live_blocks, d_hidden):
    tok_all = slot_token[0, 0]
    pick_all = slot_pick[0, 0]
    live_count = live_blocks[0, 0]
    cot_all = d_hidden[0, 0]
    hidden_width = w_gate.shape[2]
    rows_x = tokens[tok_all]
    gate_col = route_w[tok_all, pick_all]
    w_cat = jnp.concatenate((w_gate[0], w_up[0]), axis=1)
    w_full = lax.all_gather(w_cat, "dp", axis=0, tiled=True)
    hidden, grad_cat, token_grad_rows, route_grad = run_blocks(
        rows_x, gate_col, cot_all, w_full, live_count
    )
    token_grad = (
        jnp.zeros((tokens.shape[0], tokens.shape[1]), jnp.float32).at[tok_all].add(token_grad_rows)
    )
    route_part = jnp.zeros(route_w.shape, jnp.float32).at[tok_all, pick_all].add(route_grad)
    token_sum, route_sum = (
        lax.psum_scatter(
            token_grad.astype(jnp.bfloat16), "own", scatter_dimension=0, tiled=True
        ).astype(jnp.float32),
        lax.psum_scatter(
            route_part.astype(jnp.bfloat16), "own", scatter_dimension=0, tiled=True
        ).astype(jnp.float32),
    )
    summed = lax.psum_scatter(
        weight_sum(rows_x, grad_cat, live_count, 0, tokens.shape[1]),
        "dp",
        scatter_dimension=0,
        tiled=True,
    )
    grad_scale = 1.0 / math.sqrt(tokens.shape[0] * lax.axis_size("dp"))
    summed = summed * grad_scale
    return (
        hidden[None, None],
        summed[:, :hidden_width][None],
        summed[:, hidden_width:][None],
        token_sum.astype(jnp.bfloat16),
        route_sum,
    )


def solution(mesh):
    in_specs = (
        P("dp", None),
        P("dp", None),
        P("own", "dp", None),
        P("own", "dp", None),
        P("dp", "own", None),
        P("dp", "own", None),
        P("dp", "own"),
        P("dp", "own", None, None),
    )
    out_specs = (
        P("dp", "own", None, None),
        P("own", "dp", None),
        P("own", "dp", None),
        P(("dp", "own"), None),
        P(("dp", "own"), None),
    )
    return jax.shard_map(shards, mesh=mesh, in_specs=in_specs, out_specs=out_specs, check_vma=False)
```

profile of v0, /device:TPU:0, one launch (start us, length us, event | category | flops | bytes accessed | tf_op | source)
XLA Modules:
  0.0 597.1 jit_solution(12602224739103309621)
XLA Ops:
  7.2 0.0 copy-start
  7.2 0.0 all-gather.2.cloned.1.call-start
  7.2 2.2 pad_maximum_fusion.2
  9.4 0.0 all-gather.2.cloned.1.call-update
  9.4 0.0 reduce-scatter.10.cloned.1.call-start
  9.5 0.7 or_select_fusion
  10.2 0.0 copy-done
  10.2 4.8 gather_fusion.1
  15.1 8.4 %gather_fusion = bf16[512,2560]{1,0:T(8,128)(2,1)S(1)} fusion(bf16[1024,2560]{1,0:T(8,128)(2,1)} %param.12, s32[1024]{0:T(1024)S(1)} %pad_clamp_fusion), kind=kCustom, calls=%fused_computation | custom fusion | bytes 5244928 | tf_op jit(solution)/shard_map/gather | solution.py:82
  23.5 108.4 %all-gather.2.cloned.1.call-done = bf16[2560,1536]{1,0:T(8,128)(2,1)} async-done(((bf16[320,1536]{1,0:T(8,128)(2,1)}), bf16[2560,1536]{1,0:T(8,128)(2,1)}) %all-gather.2.cloned.1.call-update) | async-done | bytes 7864336 | tf_op jit(solution)/shard_map/all_gather | solution.py:85
  131.9 0.9 broadcast_in_dim.37
  132.8 1.2 broadcast_in_dim.38
  134.1 3.0 broadcast_in_dim.39
  137.1 15.8 %while.26 = (s32[]{:T(128)}, bf16[512,768]{1,0:T(8,128)(2,1)}, bf16[512,1536]{1,0:T(8,128)(2,1)}, f32[512,2560]{1,0:T(8,128)}, f32[512]{0:T(512)S(1)}, /*index=5...) while((s32[]{:T(128)}, bf16[512,768]{1,0:T(8,128)(2,1)}, ...), condition=%wide.region_2.0_spmd, body=%wide.region_0.0_spmd.sunk | while | flops 2017296256 | bytes 22023888 | solution.py:54
  137.8 0.1 dynamic_slice.31
  137.9 4.4 fusion.36
  142.3 1.2 fusion.38
  143.6 0.8 fusion.37
  144.4 0.2 dynamic_update_slice.22
  144.6 0.8 fusion.39
  145.4 6.9 %convolution_dynamic-update-slice_fusion.2 = f32[512,2560]{1,0:T(8,128)} fusion(f32[512,2560]{1,0:T(8,128)} %get-tuple-element.249, s32[]{:T(128)S(6)} %select_n.53, bf16[2560,1536]{1,0:T(8,128)(2,1)} %get-tuple-element.267, bf16[128,768]{1,0:T(8,128)(2,1)S(1)} %get-tuple-element.224, bf16[128,768]{1,0:T(8,128)(2,1)S(1)} %get-tuple-element.225), kind=kOutput, calls=%fused_computation.4.clone.1 | convolution fusion | flops 1007419392 | bytes 9568260 | tf_op jit(solution)/shard_map/while/body/dot_general | solution.py:45
  152.9 23.9 %scatter_fusion = f32[1024,2]{0,1:T(2,128)S(1)} fusion(f32[1024,2]{0,1:T(2,128)S(1)} %broadcast_in_dim.46, s32[512]{0:T(512)S(1)} %bitcast.33, f32[512]{0:T(512)S(1)} %get-tuple-element.93), kind=kCustom, calls=%fused_computation.3 | custom fusion | flops 512 | bytes 10240 | tf_op jit(solution)/shard_map/scatter-add | solution.py:92
  176.8 0.9 copy.13
  177.7 0.0 reduce-scatter.10.cloned.1.call-update
  177.7 0.0 reduce-scatter.6.cloned.1.call-start
  177.8 7.5 %broadcast_in_dim.42 = f32[2560,1536]{1,0:T(8,128)} broadcast(f32[]{:T(128)} %constant.3.clone.1), dimensions={} | broadcast | bytes 15728644 | tf_op jit(solution)/shard_map/broadcast_in_dim | solution.py:72
  185.3 14.7 %while.27 = (s32[]{:T(128)}, f32[2560,1536]{1,0:T(8,128)}, s32[]{:T(128)}, bf16[512,2560]{1,0:T(8,128)(2,1)S(1)}, bf16[512,1536]{1,0:T(8,128)(2,1)}, /*index=5*/s32[]{:T(128)}, s32[]{:T(128)}, s32[]{:T(128)}, s32[]{:T(128)}) while((s32[]{:T(128)}, f32[2560,1536]{1,0:T(8,128)}, s32[]{:T(128)}, bf16[512,2560]{1,0:T(8,128)(2,1)S(1)}, ...), condition=%wide.region_4.0_spmd, body=%wide.region_3.0_spmd.sunk | while | flops 1010565120 | bytes 32507020 | solution.py:68
  185.9 13.4 %convolution_add_fusion.2 = f32[2560,1536]{1,0:T(8,128)} fusion(f32[2560,1536]{1,0:T(8,128)} %get-tuple-element.284, bf16[512,2560]{1,0:T(8,128)(2,1)S(1)} %get-tuple-element.295, s32[]{:T(128)S(6)} %select_n.54, bf16[512,1536]{1,0:T(8,128)(2,1)} %get-tuple-element.296), kind=kOutput, calls=%fused_computation.25.clone.1 | convolution fusion | flops 1010565120 | bytes 32506880 | tf_op jit(solution)/shard_map/while/body/dot_general | solution.py:64
  200.0 0.0 reduce-scatter.6.cloned.1.call-update
  200.0 0.2 reduce-scatter.8.cloned.1.call-start
  200.2 14.4 %scatter_custom_fusion = f32[1024,2560]{1,0:T(8,128)} fusion(s32[512]{0:T(512)S(1)} %bitcast.40, f32[512,2560]{1,0:T(8,128)} %get-tuple-element.92, f32[]{:T(128)} %constant.3.clone.1), kind=kCustom, calls=%fused_computation.29 | custom fusion | flops 1310720 | bytes 10486272 | tf_op jit(solution)/shard_map/scatter-add | solution.py:90
  214.6 7.0 %convert_element_type.23 = bf16[1024,2560]{1,0:T(8,128)(2,1)} convert(f32[1024,2560]{1,0:T(8,128)} %scatter_custom_fusion) | non-fusion elementwise | flops 2621440 | bytes 15728640 | tf_op jit(solution)/shard_map/convert_element_type | solution.py:95
  221.6 0.0 reduce-scatter.8.cloned.1.call-update
  221.6 19.8 %reduce-scatter.10.cloned.1.call-done = bf16[256,2]{1,0:T(8,128)(2,1)} async-done(((bf16[1024,2]{1,0:T(8,128)(2,1)}), bf16[256,2]{1,0:T(8,128)(2,1)}) %reduce-scatter.10.cloned.1.call-update) | async-done | bytes 1040
  241.4 0.9 copy.14
  242.4 0.6 convert_element_type.25
  243.0 294.0 %reduce-scatter.6.cloned.1.call-done = f32[320,1536]{1,0:T(8,128)} async-done(((f32[2560,1536]{1,0:T(8,128)}), f32[320,1536]{1,0:T(8,128)}) %reduce-scatter.6.cloned.1.call-update) | async-done | bytes 1966096 | tf_op jit(solution)/shard_map/reduce_scatter | solution.py:101
  537.0 1.7 broadcast_multiply_fusion
  538.7 1.4 slice_bitcast_fusion
  540.1 50.5 %reduce-scatter.8.cloned.1.call-done = bf16[256,2560]{1,0:T(8,128)(2,1)} async-done(((bf16[1024,2560]{1,0:T(8,128)(2,1)}), bf16[256,2560]{1,0:T(8,128)(2,1)}) %reduce-scatter.8.cloned.1.call-update) | async-done | bytes 1310736 | tf_op jit(solution)/shard_map/reduce_scatter | solution.py:94
  (4 shorter events, 0.0 us)
Async XLA Ops:
  7.2 3.0 copy-start
  7.2 124.7 %all-gather.2.cloned.1.call-start = ((), (), s32[]{:S(2)}) async-start(), calls=%async_computation.3 | async-start | bytes 8847360 | tf_op jit(solution)/shard_map/all_gather | solution.py:85
  9.4 232.0 %reduce-scatter.10.cloned.1.call-start = ((), (), s32[]{:S(2)}) async-start(), calls=%async_computation.6 | async-start | bytes 327680
  177.7 359.3 %reduce-scatter.6.cloned.1.call-start = ((), (), s32[]{:S(2)}) async-start(), calls=%async_computation.4 | async-start | bytes 17694720 | tf_op jit(solution)/shard_map/reduce_scatter | solution.py:101
  200.0 390.6 %reduce-scatter.8.cloned.1.call-start = ((), (), s32[]{:S(2)}) async-start(), calls=%async_computation.5 | async-start | bytes 6553600 | tf_op jit(solution)/shard_map/reduce_scatter | solution.py:94
Sparse Core Ops, SparseCore 0:
  10.8 121.0 all-gather.1
  177.8 63.5 reduce-scatter.9
  245.5 291.4 reduce-scatter.5
  540.1 50.4 reduce-scatter.7
where the time goes:
time: 597 us
  waiting for transfers between devices  473 us (79%)
  other arithmetic  53.3 us (9%)
  local copies, waits for them, and re-layouts  29.4 us (5%)
  matrix products  24.7 us (4%)
  between operations  13.9 us (2%)
    reduce_scatter x1, waiting for transfers between devices, shards(): lax.psum_scatter(weight_sum(rows_x, grad_cat, live_count, 0, tokens.shape...  294 us
    all_gather x1, waiting for transfers between devices, shards(): w_full = lax.all_gather(w_cat, 'dp', axis=0, tiled=True)  108 us
    reduce_scatter x1, waiting for transfers between devices, shards(): lax.psum_scatter(token_grad.astype(jnp.bfloat16), 'own', scatter_dimensio...  50.5 us
    scatter-add x1, other arithmetic, shards(): jnp.zeros(route_w.shape, jnp.float32).at[tok_all, pick_all].add(route_grad)  23.9 us
    unnamed x5, waiting for transfers between devices  19.9 us
    scatter-add x1, other arithmetic, shards(): jnp.zeros((tokens.shape[0], tokens.shape[1]), jnp.float32).at[tok_all]  14.4 us
    dot_general x1, matrix products, add_block(): lax.dot_general(block_rows, block_dcat, (((0,), (0,)), ((), ())), preferr...  13.4 us
  transfers between devices with their start and end apart: 4, of which 4 were waited for; matrix products, arithmetic and copies ran while one was open for 10% of the time, Pallas kernels for 0%

commit v1 on v0

--- a/solution.py
+++ b/solution.py
@@ -1,11 +1,16 @@
 import math
+import functools
 
 import jax
 import jax.numpy as jnp
 from jax import lax
+from jax.experimental import pallas as pl
+from jax.experimental.pallas import tpu as pltpu
 from jax.sharding import PartitionSpec as P
 
 BLK = 128
+F32 = jnp.float32
+BF16 = jnp.bfloat16
 
 
 def finish(pre_gate, pre_up, block_gate, block_cot):
@@ -99,11 +104,11 @@
         ).astype(jnp.float32),
     )
     summed = lax.psum_scatter(
-        weight_sum(rows_x, grad_cat, live_count, 0, tokens.shape[1]),
+        weight_sum(rows_x, grad_cat, live_count, 0, tokens.shape[1]).astype(jnp.bfloat16),
         "dp",
         scatter_dimension=0,
         tiled=True,
-    )
+    ).astype(jnp.float32)
     grad_scale = 1.0 / math.sqrt(tokens.shape[0] * lax.axis_size("dp"))
     summed = summed * grad_scale
     return (
@@ -113,6 +118,350 @@
         token_sum.astype(jnp.bfloat16),
         route_sum,
     )
+
+
+def ring_pos(index, n):
+    return jnp.where(lax.rem(index, 2) == 0, index // 2, n - 1 - index // 2)
+
+
+def ring_index(pos, n):
+    return jnp.where(pos < n // 2, 2 * pos, 2 * (n - 1 - pos) + 1)
+
+
+def tile_of(size, wanted):
+    tile = wanted
+    while size % tile:
+        tile -= 128
+    return tile
+
+
+def moe_kernel(
+    n, n_own, scale,
+    live_ref, tok_col, tok_row, pick_col, route_t, tokens_hbm, wg_hbm, wu_hbm, cot_hbm,
+    hidden_ref, gg_ref, gu_ref, dtok_ref, droute_ref,
+    tokens_v, cot_v, wg_v, wu_v, x3, onehot, gcol, acc_g, acc_u, dcat_g, dcat_u,
+    rows_v, slab_out, slab_in, red_g, red_u,
+    local_sem, ag_send, ag_recv, rs_send, rs_recv, own_send, own_recv,
+):
+    cap = tok_col.shape[0]
+    n_tok, width = tokens_v.shape
+    hw = wg_v.shape[1]
+    depth = width // n
+    half = depth // 2
+    cols = hw // 2
+    part = n_tok // n_own
+    wide = rows_v.shape[1]
+    me = lax.axis_index("dp")
+    own = lax.axis_index("own")
+    pos = ring_pos(me, n)
+    right = ring_index(lax.rem(pos + 1, n), n)
+    left = ring_index(lax.rem(pos + n - 1, n), n)
+
+    def owner_of(shift):
+        return ring_index(lax.rem(pos + n + shift, n), n)
+
+    def row_start(owner, piece):
+        return pl.multiple_of(owner * depth + piece * half, half)
+
+    locals_ = (
+        pltpu.make_async_copy(tokens_hbm, tokens_v, local_sem.at[0]),
+        pltpu.make_async_copy(cot_hbm, cot_v, local_sem.at[1]),
+        pltpu.make_async_copy(wg_hbm, wg_v.at[pl.ds(row_start(me, 0), depth)], local_sem.at[2]),
+        pltpu.make_async_copy(wu_hbm, wu_v.at[pl.ds(row_start(me, 0), depth)], local_sem.at[3]),
+    )
+    for copy in locals_:
+        copy.start()
+
+    barrier = pltpu.get_barrier_semaphore()
+    for neighbour in (left, right):
+        pl.semaphore_signal(
+            barrier, inc=1, device_id=(neighbour, own), device_id_type=pl.DeviceIdType.MESH
+        )
+    for offset in range(1, n_own):
+        pl.semaphore_signal(
+            barrier, inc=1, device_id=(me, lax.rem(own + offset, n_own)),
+            device_id_type=pl.DeviceIdType.MESH,
+        )
+    pl.semaphore_wait(barrier, 1 + n_own)
+
+    def gather_copy(way, piece, step, first=False):
+        buf, peer = (wg_v, right) if way == 0 else (wu_v, left)
+        owner = owner_of(-step if way == 0 else step)
+        dst = buf.at[pl.ds(row_start(owner, piece), half)]
+        src = dst
+        if first:
+            src = (wg_hbm, wu_hbm)[way].at[pl.ds(piece * half, half)]
+        return pltpu.make_async_remote_copy(
+            src_ref=src, dst_ref=dst,
+            send_sem=ag_send.at[way, piece, step], recv_sem=ag_recv.at[way, piece, step],
+            device_id=(peer, own), device_id_type=pl.DeviceIdType.MESH,
+        )
+
+    for piece in range(2):
+        for way in range(2):
+            gather_copy(way, piece, 0, True).start()
+
+    tile = 128
+    slots = cap // tile
+
+    locals_[0].wait()
+
+    @pl.loop(0, slots)
+    def _(t):
+        r = pl.ds(pl.multiple_of(t * tile, tile), tile)
+        hit = tok_col[r, :] == lax.broadcasted_iota(jnp.int32, (tile, n_tok), 1)
+        onehot[r, :] = jnp.where(hit, 1.0, 0.0).astype(BF16)
+        chosen = jnp.where(pick_col[r, :] == 0, route_t[0:1, :], route_t[1:2, :])
+        g = jnp.sum(jnp.where(hit, chosen, 0.0), axis=1, keepdims=True)
+        gcol[r, :] = jnp.broadcast_to(g, (tile, 128))
+
+    @pl.loop(0, n // 2)
+    def _(t):
+        c = pl.ds(pl.multiple_of(t * 2 * depth, 2 * depth), 2 * depth)
+        both = jnp.dot(onehot[...], tokens_v[:, c], preferred_element_type=F32).astype(BF16)
+        x3[2 * t] = both[:, :depth]
+        x3[2 * t + 1] = both[:, depth:]
+
+    for copy in locals_[2:]:
+        copy.wait()
+    mine = pl.ds(row_start(me, 0), depth)
+    acc_g[...] = jnp.dot(x3[me], wg_v[mine, :], preferred_element_type=F32)
+    acc_u[...] = jnp.dot(x3[me], wu_v[mine, :], preferred_element_type=F32)
+
+    @pl.loop(0, n - 1)
+    def _(step):
+        for piece in range(2):
+            for way in range(2):
+                got = owner_of(-step - 1 if way == 0 else step + 1)
+                buf = (wg_v, wu_v)[way]
+                here = buf.at[pl.ds(row_start(got, piece), half)]
+                pltpu.make_async_remote_copy(
+                    src_ref=here, dst_ref=here,
+                    send_sem=ag_send.at[way, piece, step], recv_sem=ag_recv.at[way, piece, step],
+                    device_id=((left, right)[way], own), device_id_type=pl.DeviceIdType.MESH,
+                ).wait_recv()
+
+                @pl.when(step < n - 2)
+                def _():
+                    gather_copy(way, piece, step + 1).start()
+
+        og = owner_of(-step - 1)
+        ou = owner_of(step + 1)
+        acc_g[...] += jnp.dot(
+            x3[og], wg_v[pl.ds(row_start(og, 0), depth), :], preferred_element_type=F32
+        )
+        acc_u[...] += jnp.dot(
+            x3[ou], wu_v[pl.ds(row_start(ou, 0), depth), :], preferred_element_type=F32
+        )
+
+    locals_[1].wait()
+    live = live_ref[0, 0] * BLK
+    ftile = 64
+
+    @pl.loop(0, cap // ftile)
+    def _(t):
+        start = pl.multiple_of(t * ftile, ftile)
+        r = pl.ds(start, ftile)
+        a = acc_g[r, :]
+        u = acc_u[r, :]
+        g = gcol[r, 0:1]
+        cot = cot_v[r, :].astype(F32)
+        alive = (lax.broadcasted_iota(jnp.int32, (ftile, hw), 0) + start) < live
+        sig = jax.nn.sigmoid(a)
+        act = a * sig
+        hidden_ref[r, :] = jnp.where(alive, act * u * g, 0.0).astype(BF16)
+        z = cot * g
+        pa = z * u * sig * (1.0 + a * (1.0 - sig))
+        dcat_g[r, :] = jnp.where(alive, pa, 0.0).astype(BF16)
+        dcat_u[r, :] = jnp.where(alive, z * act, 0.0).astype(BF16)
+        q = jnp.sum(jnp.where(alive, cot * act * u, 0.0), axis=1, keepdims=True)
+        lane = lax.broadcasted_iota(jnp.int32, (ftile, 128), 1)
+        rows_v[r, width:] = jnp.where(lane == pick_col[r, :], q, 0.0).astype(BF16)
+
+    def term(way, owner, piece):
+        dcat = (dcat_g, dcat_u)[way]
+        return lax.dot_general(
+            x3[owner], dcat[:, piece * cols:(piece + 1) * cols], (((0,), (0,)), ((), ())),
+            preferred_element_type=F32,
+        )
+
+    def reduce_copy(way, piece, step, src_slot):
+        red, peer = (red_g, right) if way == 0 else (red_u, left)
+        return pltpu.make_async_remote_copy(
+            src_ref=red.at[src_slot, piece], dst_ref=red.at[step, piece],
+            send_sem=rs_send.at[way, piece, step], recv_sem=rs_recv.at[way, piece, step],
+            device_id=(peer, own), device_id_type=pl.DeviceIdType.MESH,
+        )
+
+    for piece in range(2):
+        for way in range(2):
+            red = (red_g, red_u)[way]
+            owner = owner_of(-1 if way == 0 else 1)
+            red[n - 1, piece] = term(way, owner, piece).astype(BF16)
+            reduce_copy(way, piece, 0, n - 1).start()
+
+    ctile = tile_of(width, 512)
+
+    @pl.loop(0, width // ctile)
+    def _(t):
+        c = pl.ds(pl.multiple_of(t * ctile, ctile), ctile)
+        dims = (((1,), (1,)), ((), ()))
+        total = lax.dot_general(dcat_g[...], wg_v[c, :], dims, preferred_element_type=F32)
+        total += lax.dot_general(dcat_u[...], wu_v[c, :], dims, preferred_element_type=F32)
+        rows_v[:, c] = total.astype(BF16)
+
+    stile = tile_of(wide, 384)
+
+    def slab_copy(offset):
+        return pltpu.make_async_remote_copy(
+            src_ref=slab_out.at[offset], dst_ref=slab_in.at[offset - 1],
+            send_sem=own_send.at[offset - 1], recv_sem=own_recv.at[offset - 1],
+            device_id=(me, lax.rem(own + offset, n_own)), device_id_type=pl.DeviceIdType.MESH,
+        )
+
+    def make_slab(offset):
+        first = lax.rem(own + offset, n_own) * part
+        hit = (lax.broadcasted_iota(jnp.int32, (part, cap), 0) + first) == tok_row[...]
+        spread = jnp.where(hit, 1.0, 0.0).astype(BF16)
+
+        @pl.loop(0, wide // stile)
+        def _(t):
+            c = pl.ds(pl.multiple_of(t * stile, stile), stile)
+            slab_out[offset, :, c] = jnp.dot(
+                spread, rows_v[:, c], preferred_element_type=F32
+            ).astype(BF16)
+
+    for offset in range(1, n_own):
+        make_slab(offset)
+        slab_copy(offset).start()
+
+    @pl.loop(1, n - 1)
+    def _(step):
+        for piece in range(2):
+            for way in range(2):
+                red = (red_g, red_u)[way]
+                owner = owner_of(-1 - step if way == 0 else 1 + step)
+                add = term(way, owner, piece)
+                reduce_copy(way, piece, step - 1, step - 1).wait_recv()
+                red[step - 1, piece] = (red[step - 1, piece].astype(F32) + add).astype(BF16)
+                reduce_copy(way, piece, step, step - 1).start()
+
+    make_slab(0)
+
+    for piece in range(2):
+        for way in range(2):
+            red = (red_g, red_u)[way]
+            out = (gg_ref, gu_ref)[way]
+            add = term(way, me, piece)
+            reduce_copy(way, piece, n - 2, n - 2).wait_recv()
+            out[:, piece * cols:(piece + 1) * cols] = (
+                red[n - 2, piece].astype(F32) + add
+            ) * scale
+
+    for offset in range(1, n_own):
+        slab_copy(offset).wait_recv()
+
+    def slab_sum(c):
+        total = slab_out[0, :, c].astype(F32)
+        for k in range(n_own - 1):
+            total = total + slab_in[k, :, c].astype(F32)
+        return total
+
+    @pl.loop(0, width // ctile)
+    def _(t):
+        c = pl.ds(pl.multiple_of(t * ctile, ctile), ctile)
+        dtok_ref[:, c] = slab_sum(c).astype(BF16)
+
+    droute_ref[...] = slab_sum(pl.ds(width, 128))
+
+    for offset in range(1, n_own):
+        slab_copy(offset).wait_send()
+
+    for piece in range(2):
+        for way in range(2):
+            gather_copy(way, piece, 0, True).wait_send()
+            reduce_copy(way, piece, 0, n - 1).wait_send()
+
+    @pl.loop(1, n - 1)
+    def _(step):
+        for piece in range(2):
+            for way in range(2):
+                gather_copy(way, piece, step).wait_send()
+                reduce_copy(way, piece, step, step - 1).wait_send()
+
+
+def fused(n, n_own, tokens, route_w, w_gate, w_up, slot_token, slot_pick, live_blocks, d_hidden):
+    n_tok, width = tokens.shape
+    depth, hw = w_gate.shape[1:]
+    cap = slot_token.shape[2]
+    part = n_tok // n_own
+    scale = 1.0 / math.sqrt(n_tok * n)
+    vmem = pl.BlockSpec(memory_space=pltpu.VMEM)
+    hbm = pl.BlockSpec(memory_space=pl.ANY)
+    flops = 6 * cap * width * 2 * hw
+    outs = pl.pallas_call(
+        functools.partial(moe_kernel, n, n_own, scale),
+        out_shape=(
+            jax.ShapeDtypeStruct((cap, hw), BF16),
+            jax.ShapeDtypeStruct((depth, hw), F32),
+            jax.ShapeDtypeStruct((depth, hw), F32),
+            jax.ShapeDtypeStruct((part, width), BF16),
+            jax.ShapeDtypeStruct((part, 128), F32),
+        ),
+        in_specs=[pl.BlockSpec(memory_space=pltpu.SMEM)] + [vmem] * 4 + [hbm] * 4,
+        out_specs=[vmem] * 5,
+        scratch_shapes=[
+            pltpu.VMEM((n_tok, width), BF16),
+            pltpu.VMEM((cap, hw), BF16),
+            pltpu.VMEM((width, hw), BF16),
+            pltpu.VMEM((width, hw), BF16),
+            pltpu.VMEM((n, cap, depth), BF16),
+            pltpu.VMEM((cap, n_tok), BF16),
+            pltpu.VMEM((cap, 128), F32),
+            pltpu.VMEM((cap, hw), F32),
+            pltpu.VMEM((cap, hw), F32),
+            pltpu.VMEM((cap, hw), BF16),
+            pltpu.VMEM((cap, hw), BF16),
+            pltpu.VMEM((cap, width + 128), BF16),
+            pltpu.VMEM((n_own, part, width + 128), BF16),
+            pltpu.VMEM((n_own - 1, part, width + 128), BF16),
+            pltpu.VMEM((n, 2, depth, hw // 2), BF16),
+            pltpu.VMEM((n, 2, depth, hw // 2), BF16),
+            pltpu.SemaphoreType.DMA((4,)),
+            pltpu.SemaphoreType.DMA((2, 2, n - 1)),
+            pltpu.SemaphoreType.DMA((2, 2, n - 1)),
+            pltpu.SemaphoreType.DMA((2, 2, n - 1)),
+            pltpu.SemaphoreType.DMA((2, 2, n - 1)),
+            pltpu.SemaphoreType.DMA((n_own - 1,)),
+            pltpu.SemaphoreType.DMA((n_own - 1,)),
+        ],
+        compiler_params=pltpu.CompilerParams(
+            collective_id=0, has_side_effects=True, vmem_limit_bytes=60 * 1024 * 1024
+        ),
+        cost_estimate=pl.CostEstimate(
+            flops=flops, bytes_accessed=16 * 1024 * 1024, transcendentals=cap * hw
+        ),
+    )(
+        live_blocks, slot_token.reshape(cap, 1), slot_token.reshape(1, cap),
+        slot_pick.reshape(cap, 1), route_w.T, tokens, w_gate[0], w_up[0], d_hidden[0, 0],
+    )
+    hidden, grad_gate, grad_up, d_tokens, d_route = outs
+    return (
+        hidden[None, None], grad_gate[None], grad_up[None], d_tokens,
+        d_route[:, : route_w.shape[1]],
+    )
+
+
+def local_part(n, n_own, *args):
+    depth, hw = args[2].shape[1:]
+    cap = args[4].shape[2]
+    fits = (
+        n % 2 == 0 and n > 3 and n_own > 1 and depth % 64 == 0 and hw % 256 == 0
+        and cap % 128 == 0 and args[0].shape[0] % (128 * n_own) == 0 and args[1].shape[1] == 2
+    )
+    if fits:
+        return fused(n, n_own, *args)
+    return shards(*args)
 
 
 def solution(mesh):
@@ -133,4 +482,5 @@
         P(("dp", "own"), None),
         P(("dp", "own"), None),
     )
-    return jax.shard_map(shards, mesh=mesh, in_specs=in_specs, out_specs=out_specs, check_vma=False)
+    body = functools.partial(local_part, mesh.shape["dp"], mesh.shape["own"])
+    return jax.shard_map(body, mesh=mesh, in_specs=in_specs, out_specs=out_specs, check_vma=False)

time: 597 us -> 179 us (0.30)
  waiting for transfers between devices: 473 us -> 0 us
  Pallas kernels: 0 us -> 166 us
  other arithmetic: 53.3 us -> 0 us
  matrix products: 24.7 us -> 0 us
  local copies, waits for them, and re-layouts: 29.4 us -> 11.1 us
  between operations: 13.9 us -> 1.3 us
    reduce_scatter x2 -> x0, waiting for transfers between devices: 345 us -> none  [the longest x1 294 us: shards(): lax.psum_scatter(weight_sum(rows_x, grad_cat, live_count, 0, tokens.shape...]
    pallas_call x0 -> x1, Pallas kernels: none -> 166 us  [fused(): pl.pallas_call(functools.partial(moe_kernel, n, n_own, scale), out_shape=...]
    all_gather x1 -> x0, waiting for transfers between devices: 108 us -> none  [shards(): w_full = lax.all_gather(w_cat, 'dp', axis=0, tiled=True)]
    scatter-add x2 -> x0, other arithmetic: 38.2 us -> none  [the longest x1 23.9 us: shards(): jnp.zeros(route_w.shape, jnp.float32).at[tok_all, pick_all].add(route_grad)]
    dot_general x3 -> x0, matrix products: 24.7 us -> none  [the longest x1 13.4 us: add_block(): lax.dot_general(block_rows, block_dcat, (((0,), (0,)), ((), ())), preferr...]
    unnamed x5 -> x0, waiting for transfers between devices: 19.9 us -> none
    broadcast_in_dim x7 -> x0, local copies, waits for them, and re-layouts: 14.1 us -> none  [the longest x1 7.51 us: weight_sum(): jnp.zeros((length, grad_cat.shape[1]), jnp.float32)]
    gather x2 -> x0, local copies, waits for them, and re-layouts: 13.2 us -> none  [the longest x1 8.38 us: shards(): rows_x = tokens[tok_all]]
  transfers between devices with their start and end apart: 4 -> 0, of which waited for: 4 -> 0; matrix products, arithmetic and copies ran while one was open for 10% -> 0% of each run, Pallas kernels for 0% -> 0%
where the time goes in v1:
time: 179 us
  Pallas kernels  166 us (93%)
  local copies, waits for them, and re-layouts  11.1 us (6%)
    pallas_call x1, Pallas kernels, fused(): pl.pallas_call(functools.partial(moe_kernel, n, n_own, scale), out_shape=...  166 us
    unnamed x11, local copies, waits for them, and re-layouts  7.99 us

profile of v1, /device:TPU:0, one launch (start us, length us, event | category | flops | bytes accessed | tf_op | source)
XLA Modules:
  0.0 178.6 jit_solution(5868483019511060669)
XLA Ops:
  1.3 1.5 copy.15.pick_col
  2.8 1.5 copy.14.tok_col
  4.3 166.2 %shard_map.119 = (bf16[512,768]{1,0:T(8,128)(2,1)}, f32[320,768]{1,0:T(8,128)}, f32[320,768]{1,0:T(8,128)}, bf16[256,2560]{1,0:T(8,128)(2,1)}, f32[256,128]{1,0:T(8,128)}) custom-call(s32[1,1]{1,0:T(1,128)S(6)} %copy.21.live_ref, s32[512,1]{1,0:T(8,128)} %copy.14.tok_col, s32[1,512]{1,0:T(1,128)} %bitcast.17, s32[512,1]{1,0:T(8,128)} %copy.15.pick_col, ...), custom_call_target="tpu_custom_call" | custom-call | flops 12079595520 | bytes 16777216 | tf_op jit(solution)/shard_map/pallas_call | solution.py:402
  170.6 0.0 copy-start.2
  170.6 1.6 copy.16
  172.3 2.1 %copy.22 = bf16[1,1,512,768]{3,2,1,0:T(8,128)(2,1)} copy(bf16[1,1,512,768]{3,2,1,0:T(8,128)(2,1)} %bitcast.13) | data formatting | bytes 1572864
  174.3 0.0 copy-done.2
  174.3 0.0 copy-start.1
  174.3 0.9 copy.23
  175.3 0.6 copy-done.1
  175.9 0.0 copy-start
  175.9 0.9 copy.24
  176.8 0.7 copy-done
  177.6 1.1 copy.25
Async XLA Ops:
  170.6 3.7 %copy-start.2 = (f32[320,768]{1,0:T(8,128)S(1)}, f32[320,768]{1,0:T(8,128)}, u32[]{:S(2)}) copy-start(f32[320,768]{1,0:T(8,128)} %get-tuple-element.11) | copy-start | bytes 2949124
  174.3 1.6 copy-start.1
  175.9 1.7 copy-start

commit v2 on v1

--- a/solution.py
+++ b/solution.py
@@ -137,17 +137,17 @@
 
 def moe_kernel(
     n, n_own, scale,
-    live_ref, tok_col, tok_row, pick_col, route_t, tokens_hbm, wg_hbm, wu_hbm, cot_hbm,
-    hidden_ref, gg_ref, gu_ref, dtok_ref, droute_ref,
+    live_ref, tok_row, pick_row, route_t, tokens_hbm, wg_hbm, wu_hbm, cot_hbm,
+    hidden_hbm, gg_ref, gu_ref, dtok_hbm, droute_ref,
+    hidden_ref, dtok_ref, pick_col, qsum,
     tokens_v, cot_v, wg_v, wu_v, x3, onehot, gcol, acc_g, acc_u, dcat_g, dcat_u,
     rows_v, slab_out, slab_in, red_g, red_u,
     local_sem, ag_send, ag_recv, rs_send, rs_recv, own_send, own_recv,
 ):
-    cap = tok_col.shape[0]
+    cap = tok_row.shape[1]
     n_tok, width = tokens_v.shape
     hw = wg_v.shape[1]
     depth = width // n
-    half = depth // 2
     cols = hw // 2
     part = n_tok // n_own
     wide = rows_v.shape[1]
@@ -160,14 +160,17 @@
     def owner_of(shift):
         return ring_index(lax.rem(pos + n + shift, n), n)
 
-    def row_start(owner, piece):
-        return pl.multiple_of(owner * depth + piece * half, half)
+    def rows_of(owner):
+        return pl.ds(pl.multiple_of(owner * depth, depth), depth)
+
+    def cols_of(piece):
+        return pl.ds(piece * cols, cols)
 
     locals_ = (
         pltpu.make_async_copy(tokens_hbm, tokens_v, local_sem.at[0]),
         pltpu.make_async_copy(cot_hbm, cot_v, local_sem.at[1]),
-        pltpu.make_async_copy(wg_hbm, wg_v.at[pl.ds(row_start(me, 0), depth)], local_sem.at[2]),
-        pltpu.make_async_copy(wu_hbm, wu_v.at[pl.ds(row_start(me, 0), depth)], local_sem.at[3]),
+        pltpu.make_async_copy(wg_hbm, wg_v.at[rows_of(me)], local_sem.at[2]),
+        pltpu.make_async_copy(wu_hbm, wu_v.at[rows_of(me)], local_sem.at[3]),
     )
     for copy in locals_:
         copy.start()
@@ -187,33 +190,61 @@
     def gather_copy(way, piece, step, first=False):
         buf, peer = (wg_v, right) if way == 0 else (wu_v, left)
         owner = owner_of(-step if way == 0 else step)
-        dst = buf.at[pl.ds(row_start(owner, piece), half)]
+        dst = buf.at[rows_of(owner), cols_of(piece)]
         src = dst
         if first:
-            src = (wg_hbm, wu_hbm)[way].at[pl.ds(piece * half, half)]
+            src = (wg_hbm, wu_hbm)[way].at[:, cols_of(piece)]
         return pltpu.make_async_remote_copy(
             src_ref=src, dst_ref=dst,
             send_sem=ag_send.at[way, piece, step], recv_sem=ag_recv.at[way, piece, step],
             device_id=(peer, own), device_id_type=pl.DeviceIdType.MESH,
         )
 
-    for piece in range(2):
-        for way in range(2):
-            gather_copy(way, piece, 0, True).start()
+    for way in range(2):
+        gather_copy(way, 0, 0, True).start()
 
     tile = 128
-    slots = cap // tile
-
     locals_[0].wait()
 
-    @pl.loop(0, slots)
+    @pl.loop(0, cap // tile)
     def _(t):
         r = pl.ds(pl.multiple_of(t * tile, tile), tile)
-        hit = tok_col[r, :] == lax.broadcasted_iota(jnp.int32, (tile, n_tok), 1)
+        token = jnp.broadcast_to(tok_row[:, r], (tile, tile)).T
+        pick = jnp.broadcast_to(pick_row[:, r], (tile, tile)).T
+        pick_col[r, :] = pick
+        hit = token[:, 0:1] == lax.broadcasted_iota(jnp.int32, (tile, n_tok), 1)
         onehot[r, :] = jnp.where(hit, 1.0, 0.0).astype(BF16)
-        chosen = jnp.where(pick_col[r, :] == 0, route_t[0:1, :], route_t[1:2, :])
+        chosen = jnp.where(pick[:, 0:1] == 0, route_t[0:1, :], route_t[1:2, :])
         g = jnp.sum(jnp.where(hit, chosen, 0.0), axis=1, keepdims=True)
         gcol[r, :] = jnp.broadcast_to(g, (tile, 128))
+
+    def owners_at(step):
+        return owner_of(-step - 1), owner_of(step + 1)
+
+    def take(piece, step):
+        for way in range(2):
+            here = (wg_v, wu_v)[way].at[rows_of(owners_at(step)[way]), cols_of(piece)]
+            pltpu.make_async_remote_copy(
+                src_ref=here, dst_ref=here,
+                send_sem=ag_send.at[way, piece, step], recv_sem=ag_recv.at[way, piece, step],
+                device_id=((left, right)[way], own), device_id_type=pl.DeviceIdType.MESH,
+            ).wait_recv()
+
+            @pl.when(step < n - 2)
+            def _():
+                gather_copy(way, piece, step + 1).start()
+
+    def accumulate(piece, step):
+        for way in range(2):
+            owner = owners_at(step)[way]
+            acc = (acc_g, acc_u)[way]
+            acc[:, cols_of(piece)] += jnp.dot(
+                x3[owner], (wg_v, wu_v)[way][rows_of(owner), cols_of(piece)],
+                preferred_element_type=F32,
+            )
+
+    lag = 2
+    take(0, 0)
 
     @pl.loop(0, n // 2)
     def _(t):
@@ -222,61 +253,53 @@
         x3[2 * t] = both[:, :depth]
         x3[2 * t + 1] = both[:, depth:]
 
+    take(0, 1)
+    for way in range(2):
+        gather_copy(way, 1, 0, True).start()
     for copy in locals_[2:]:
         copy.wait()
-    mine = pl.ds(row_start(me, 0), depth)
-    acc_g[...] = jnp.dot(x3[me], wg_v[mine, :], preferred_element_type=F32)
-    acc_u[...] = jnp.dot(x3[me], wu_v[mine, :], preferred_element_type=F32)
-
-    @pl.loop(0, n - 1)
+    acc_g[...] = jnp.dot(x3[me], wg_v[rows_of(me), :], preferred_element_type=F32)
+    acc_u[...] = jnp.dot(x3[me], wu_v[rows_of(me), :], preferred_element_type=F32)
+    for step in range(lag):
+        accumulate(0, step)
+
+    @pl.loop(lag, n - 1)
     def _(step):
-        for piece in range(2):
-            for way in range(2):
-                got = owner_of(-step - 1 if way == 0 else step + 1)
-                buf = (wg_v, wu_v)[way]
-                here = buf.at[pl.ds(row_start(got, piece), half)]
-                pltpu.make_async_remote_copy(
-                    src_ref=here, dst_ref=here,
-                    send_sem=ag_send.at[way, piece, step], recv_sem=ag_recv.at[way, piece, step],
-                    device_id=((left, right)[way], own), device_id_type=pl.DeviceIdType.MESH,
-                ).wait_recv()
-
-                @pl.when(step < n - 2)
-                def _():
-                    gather_copy(way, piece, step + 1).start()
-
-        og = owner_of(-step - 1)
-        ou = owner_of(step + 1)
-        acc_g[...] += jnp.dot(
-            x3[og], wg_v[pl.ds(row_start(og, 0), depth), :], preferred_element_type=F32
-        )
-        acc_u[...] += jnp.dot(
-            x3[ou], wu_v[pl.ds(row_start(ou, 0), depth), :], preferred_element_type=F32
-        )
+        take(0, step)
+        take(1, step - lag)
+        accumulate(0, step)
+        accumulate(1, step - lag)
 
     locals_[1].wait()
     live = live_ref[0, 0] * BLK
     ftile = 64
 
-    @pl.loop(0, cap // ftile)
-    def _(t):
-        start = pl.multiple_of(t * ftile, ftile)
-        r = pl.ds(start, ftile)
-        a = acc_g[r, :]
-        u = acc_u[r, :]
-        g = gcol[r, 0:1]
-        cot = cot_v[r, :].astype(F32)
-        alive = (lax.broadcasted_iota(jnp.int32, (ftile, hw), 0) + start) < live
-        sig = jax.nn.sigmoid(a)
-        act = a * sig
-        hidden_ref[r, :] = jnp.where(alive, act * u * g, 0.0).astype(BF16)
-        z = cot * g
-        pa = z * u * sig * (1.0 + a * (1.0 - sig))
-        dcat_g[r, :] = jnp.where(alive, pa, 0.0).astype(BF16)
-        dcat_u[r, :] = jnp.where(alive, z * act, 0.0).astype(BF16)
-        q = jnp.sum(jnp.where(alive, cot * act * u, 0.0), axis=1, keepdims=True)
-        lane = lax.broadcasted_iota(jnp.int32, (ftile, 128), 1)
-        rows_v[r, width:] = jnp.where(lane == pick_col[r, :], q, 0.0).astype(BF16)
+    def finish_piece(piece):
+        @pl.loop(0, cap // ftile)
+        def _(t):
+            start = pl.multiple_of(t * ftile, ftile)
+            r = pl.ds(start, ftile)
+            c = cols_of(piece)
+            a = acc_g[r, c]
+            u = acc_u[r, c]
+            g = gcol[r, 0:1]
+            cot = cot_v[r, c].astype(F32)
+            alive = (lax.broadcasted_iota(jnp.int32, (ftile, cols), 0) + start) < live
+            sig = jax.nn.sigmoid(a)
+            act = a * sig
+            hidden_ref[r, c] = jnp.where(alive, act * u * g, 0.0).astype(BF16)
+            z = cot * g
+            pa = z * u * sig * (1.0 + a * (1.0 - sig))
+            dcat_g[r, c] = jnp.where(alive, pa, 0.0).astype(BF16)
+            dcat_u[r, c] = jnp.where(alive, z * act, 0.0).astype(BF16)
+            q = jnp.sum(jnp.where(alive, cot * act * u, 0.0), axis=1, keepdims=True)
+            if piece == 0:
+                qsum[r, :] = jnp.broadcast_to(q, (ftile, 128))
+            else:
+                lane = lax.broadcasted_iota(jnp.int32, (ftile, 128), 1)
+                rows_v[r, width:] = jnp.where(
+                    lane == pick_col[r, :], qsum[r, :] + q, 0.0
+                ).astype(BF16)
 
     def term(way, owner, piece):
         dcat = (dcat_g, dcat_u)[way]
@@ -293,12 +316,25 @@
             device_id=(peer, own), device_id_type=pl.DeviceIdType.MESH,
         )
 
-    for piece in range(2):
+    def reduce_first(piece):
         for way in range(2):
             red = (red_g, red_u)[way]
             owner = owner_of(-1 if way == 0 else 1)
             red[n - 1, piece] = term(way, owner, piece).astype(BF16)
             reduce_copy(way, piece, 0, n - 1).start()
+
+    finish_piece(0)
+    reduce_first(0)
+
+    @pl.loop(n - 1 - lag, n - 1)
+    def _(step):
+        take(1, step)
+        accumulate(1, step)
+
+    finish_piece(1)
+    reduce_first(1)
+    hidden_out = pltpu.make_async_copy(hidden_ref, hidden_hbm, local_sem.at[4])
+    hidden_out.start()
 
     ctile = tile_of(width, 512)
 
@@ -331,12 +367,7 @@
                 spread, rows_v[:, c], preferred_element_type=F32
             ).astype(BF16)
 
-    for offset in range(1, n_own):
-        make_slab(offset)
-        slab_copy(offset).start()
-
-    @pl.loop(1, n - 1)
-    def _(step):
+    def reduce_step(step):
         for piece in range(2):
             for way in range(2):
                 red = (red_g, red_u)[way]
@@ -346,7 +377,38 @@
                 red[step - 1, piece] = (red[step - 1, piece].astype(F32) + add).astype(BF16)
                 reduce_copy(way, piece, step, step - 1).start()
 
+    mixed = min(n - 2, n_own - 1)
+    for offset in range(1, mixed + 1):
+        reduce_step(offset)
+        make_slab(offset)
+        slab_copy(offset).start()
+    for offset in range(mixed + 1, n_own):
+        make_slab(offset)
+        slab_copy(offset).start()
+
+    @pl.loop(mixed + 1, n - 1)
+    def _(step):
+        reduce_step(step)
+
     make_slab(0)
+
+    for offset in range(1, n_own):
+        slab_copy(offset).wait_recv()
+
+    def slab_sum(c):
+        total = slab_out[0, :, c].astype(F32)
+        for k in range(n_own - 1):
+            total = total + slab_in[k, :, c].astype(F32)
+        return total
+
+    @pl.loop(0, width // ctile)
+    def _(t):
+        c = pl.ds(pl.multiple_of(t * ctile, ctile), ctile)
+        dtok_ref[:, c] = slab_sum(c).astype(BF16)
+
+    droute_ref[...] = slab_sum(pl.ds(width, 128)).T[0:droute_ref.shape[0], :]
+    dtok_out = pltpu.make_async_copy(dtok_ref, dtok_hbm, local_sem.at[5])
+    dtok_out.start()
 
     for piece in range(2):
         for way in range(2):
@@ -358,22 +420,8 @@
                 red[n - 2, piece].astype(F32) + add
             ) * scale
 
-    for offset in range(1, n_own):
-        slab_copy(offset).wait_recv()
-
-    def slab_sum(c):
-        total = slab_out[0, :, c].astype(F32)
-        for k in range(n_own - 1):
-            total = total + slab_in[k, :, c].astype(F32)
-        return total
-
-    @pl.loop(0, width // ctile)
-    def _(t):
-        c = pl.ds(pl.multiple_of(t * ctile, ctile), ctile)
-        dtok_ref[:, c] = slab_sum(c).astype(BF16)
-
-    droute_ref[...] = slab_sum(pl.ds(width, 128))
-
+    hidden_out.wait()
+    dtok_out.wait()
     for offset in range(1, n_own):
         slab_copy(offset).wait_send()
 
@@ -388,6 +436,14 @@
             for way in range(2):
                 gather_copy(way, piece, step).wait_send()
                 reduce_copy(way, piece, step, step - 1).wait_send()
+
+
+def place_kernel(*refs):
+    copies = [pltpu.make_async_copy(refs[k], refs[5 + k], refs[10].at[k]) for k in range(5)]
+    for copy in copies:
+        copy.start()
+    for copy in copies:
+        copy.wait()
 
 
 def fused(n, n_own, tokens, route_w, w_gate, w_up, slot_token, slot_pick, live_blocks, d_hidden):
@@ -406,11 +462,15 @@
             jax.ShapeDtypeStruct((depth, hw), F32),
             jax.ShapeDtypeStruct((depth, hw), F32),
             jax.ShapeDtypeStruct((part, width), BF16),
-            jax.ShapeDtypeStruct((part, 128), F32),
+            jax.ShapeDtypeStruct((route_w.shape[1], part), F32),
         ),
-        in_specs=[pl.BlockSpec(memory_space=pltpu.SMEM)] + [vmem] * 4 + [hbm] * 4,
-        out_specs=[vmem] * 5,
+        in_specs=[pl.BlockSpec(memory_space=pltpu.SMEM)] + [vmem] * 3 + [hbm] * 4,
+        out_specs=[hbm, vmem, vmem, hbm, vmem],
         scratch_shapes=[
+            pltpu.VMEM((cap, hw), BF16),
+            pltpu.VMEM((part, width), BF16),
+            pltpu.VMEM((cap, 128), jnp.int32),
+            pltpu.VMEM((cap, 128), F32),
             pltpu.VMEM((n_tok, width), BF16),
             pltpu.VMEM((cap, hw), BF16),
             pltpu.VMEM((width, hw), BF16),
@@ -427,7 +487,7 @@
             pltpu.VMEM((n_own - 1, part, width + 128), BF16),
             pltpu.VMEM((n, 2, depth, hw // 2), BF16),
             pltpu.VMEM((n, 2, depth, hw // 2), BF16),
-            pltpu.SemaphoreType.DMA((4,)),
+            pltpu.SemaphoreType.DMA((6,)),
             pltpu.SemaphoreType.DMA((2, 2, n - 1)),
             pltpu.SemaphoreType.DMA((2, 2, n - 1)),
             pltpu.SemaphoreType.DMA((2, 2, n - 1)),
@@ -442,13 +502,21 @@
             flops=flops, bytes_accessed=16 * 1024 * 1024, transcendentals=cap * hw
         ),
     )(
-        live_blocks, slot_token.reshape(cap, 1), slot_token.reshape(1, cap),
-        slot_pick.reshape(cap, 1), route_w.T, tokens, w_gate[0], w_up[0], d_hidden[0, 0],
-    )
-    hidden, grad_gate, grad_up, d_tokens, d_route = outs
+        live_blocks, slot_token.reshape(1, cap), slot_pick.reshape(1, cap), route_w.T, tokens, w_gate[0], w_up[0], d_hidden[0, 0],
+    )
+    hidden, grad_gate, grad_up, d_tokens, d_route = pl.pallas_call(
+        place_kernel,
+        out_shape=tuple(jax.ShapeDtypeStruct(o.shape, o.dtype) for o in outs),
+        in_specs=[hbm] * 5,
+        out_specs=[hbm] * 5,
+        scratch_shapes=[pltpu.SemaphoreType.DMA((5,))],
+        cost_estimate=pl.CostEstimate(
+            flops=0, bytes_accessed=8 * 1024 * 1024, transcendentals=0
+        ),
+    )(*outs)
     return (
         hidden[None, None], grad_gate[None], grad_up[None], d_tokens,
-        d_route[:, : route_w.shape[1]],
+        d_route.T,
     )
 
 

time: 179 us -> 290 us (1.62)
  Pallas kernels: 166 us -> 288 us
  local copies, waits for them, and re-layouts: 11.1 us -> 0 us
    pallas_call x0 -> x1, Pallas kernels: none -> 124 us  [fused(): pl.pallas_call(place_kernel, out_shape=tuple((jax.ShapeDtypeStruct(o.shap...]
    unnamed x11 -> x0, local copies, waits for them, and re-layouts: 7.99 us -> none
    reshape x2 -> x0, local copies, waits for them, and re-layouts: 3.07 us -> none  [the longest x1 1.54 us: fused(): slot_pick.reshape(cap, 1)]
where the time goes in v2:
time: 290 us; the launch traced here: 289 us
  Pallas kernels  288 us (99%)
    pallas_call x1, Pallas kernels, fused(): pl.pallas_call(functools.partial(moe_kernel, n, n_own, scale), out_shape=...  164 us
    pallas_call x1, Pallas kernels, fused(): pl.pallas_call(place_kernel, out_shape=tuple((jax.ShapeDtypeStruct(o.shap...  124 us

profile of v2, /device:TPU:0, one launch (start us, length us, event | category | flops | bytes accessed | tf_op | source)
XLA Modules:
  0.0 289.4 jit_solution(10458555947843655031)
XLA Ops:
  1.3 163.8 %shard_map.119 = (bf16[512,768]{1,0:T(8,128)(2,1)}, f32[320,768]{1,0:T(8,128)}, f32[320,768]{1,0:T(8,128)}, bf16[256,2560]{1,0:T(8,128)(2,1)}, f32[2,256]{1,0:T(2,128)}) custom-call(s32[1,1]{1,0:T(1,128)S(6)} %copy.13.live_ref, s32[1,512]{1,0:T(1,128)} %bitcast.17, s32[1,512]{1,0:T(1,128)} %bitcast.18, f32[2,1024]{1,0:T(2,128)} %bitcast.16, ...), custom_call_target="tpu_custom_call" | custom-call | flops 12079595520 | bytes 16777216 | tf_op jit(solution)/shard_map/pallas_call | solution.py:458
  165.1 124.3 %shard_map.120 = (bf16[512,768]{1,0:T(8,128)(2,1)}, f32[320,768]{1,0:T(8,128)}, f32[320,768]{1,0:T(8,128)}, bf16[256,2560]{1,0:T(8,128)(2,1)}, f32[2,256]{1,0:T(2,128)}) custom-call(bf16[512,768]{1,0:T(8,128)(2,1)} %get-tuple-element.15.refs_0_, f32[320,768]{1,0:T(8,128)} %get-tuple-element.16.refs_1_, f32[320,768]{1,0:T(8,128)} %get-tuple-element.17.refs_2_, ...), custom_call_target="tpu_custom_call" | custom-call | bytes 8388608 | tf_op jit(solution)/shard_map/pallas_call | solution.py:507

commit v3 on v2

--- a/solution.py
+++ b/solution.py
@@ -439,10 +439,15 @@
 
 
 def place_kernel(*refs):
-    copies = [pltpu.make_async_copy(refs[k], refs[5 + k], refs[10].at[k]) for k in range(5)]
-    for copy in copies:
+    sems = refs[15]
+    into = [pltpu.make_async_copy(refs[k], refs[10 + k], sems.at[0, k]) for k in range(5)]
+    out = [pltpu.make_async_copy(refs[10 + k], refs[5 + k], sems.at[1, k]) for k in range(5)]
+    for copy in into:
         copy.start()
-    for copy in copies:
+    for k in range(5):
+        into[k].wait()
+        out[k].start()
+    for copy in out:
         copy.wait()
 
 
@@ -509,7 +514,9 @@
         out_shape=tuple(jax.ShapeDtypeStruct(o.shape, o.dtype) for o in outs),
         in_specs=[hbm] * 5,
         out_specs=[hbm] * 5,
-        scratch_shapes=[pltpu.SemaphoreType.DMA((5,))],
+        scratch_shapes=[pltpu.VMEM(o.shape, o.dtype) for o in outs]
+        + [pltpu.SemaphoreType.DMA((2, 5))],
+        compiler_params=pltpu.CompilerParams(vmem_limit_bytes=32 * 1024 * 1024),
         cost_estimate=pl.CostEstimate(
             flops=0, bytes_accessed=8 * 1024 * 1024, transcendentals=0
         ),

time: 290 us -> 174 us (0.60)
  Pallas kernels: 288 us -> 167 us
  local copies, waits for them, and re-layouts: 0 us -> 5.51 us
    pallas_call x1, Pallas kernels: 124 us -> 2.8 us  [fused(): pl.pallas_call(place_kernel, out_shape=tuple((jax.ShapeDtypeStruct(o.shap...]
    unnamed x0 -> x10, local copies, waits for them, and re-layouts: none -> 5.51 us
where the time goes in v3:
time: 174 us; the launch traced here: 173 us
  Pallas kernels  167 us (96%)
  local copies, waits for them, and re-layouts  5.51 us (3%)
    pallas_call x1, Pallas kernels, fused(): pl.pallas_call(functools.partial(moe_kernel, n, n_own, scale), out_shape=...  164 us
    unnamed x10, local copies, waits for them, and re-layouts  5.51 us

profile of v3, /device:TPU:0, one launch (start us, length us, event | category | flops | bytes accessed | tf_op | source)
XLA Modules:
  0.0 173.4 jit_solution(5168383728897862382)
XLA Ops:
  1.3 163.8 %shard_map.119 = (bf16[512,768]{1,0:T(8,128)(2,1)}, f32[320,768]{1,0:T(8,128)}, f32[320,768]{1,0:T(8,128)}, bf16[256,2560]{1,0:T(8,128)(2,1)}, f32[2,256]{1,0:T(2,128)}) custom-call(s32[1,1]{1,0:T(1,128)S(6)} %copy.13.live_ref, s32[1,512]{1,0:T(1,128)} %bitcast.17, s32[1,512]{1,0:T(1,128)} %bitcast.18, f32[2,1024]{1,0:T(2,128)} %bitcast.16, ...), custom_call_target="tpu_custom_call" | custom-call | flops 12079595520 | bytes 16777216 | tf_op jit(solution)/shard_map/pallas_call | solution.py:463
  165.1 0.0 copy-start
  165.1 1.3 copy-done
  166.4 0.0 copy-start.1
  166.4 1.2 copy-done.1
  167.6 0.0 copy-start.2
  167.6 1.2 copy-done.2
  168.8 0.0 copy-start.3
  168.8 1.1 copy-done.3
  169.9 0.0 copy-start.4
  169.9 0.7 copy-done.4
  170.6 2.8 %shard_map.120 = (bf16[512,768]{1,0:T(8,128)(2,1)}, f32[320,768]{1,0:T(8,128)}, f32[320,768]{1,0:T(8,128)}, bf16[256,2560]{1,0:T(8,128)(2,1)}, f32[2,256]{1,0:T(2,128)}) custom-call(bf16[512,768]{1,0:T(8,128)(2,1)S(1)} %copy-done.3, f32[320,768]{1,0:T(8,128)S(1)} %copy-done.1, f32[320,768]{1,0:T(8,128)S(1)} %copy-done.2, bf16[256,2560]{1,0:T(8,128)(2,1)S(1)} %copy-done, ...), custom_call_target="tpu_custom_call" | custom-call | bytes 8388608 | tf_op jit(solution)/shard_map/pallas_call | solution.py:512
Async XLA Ops:
  165.1 1.3 copy-start
  166.4 1.2 copy-start.1
  167.6 1.2 copy-start.2
  168.8 1.1 copy-start.3
  169.9 0.7 copy-start.4
